TPU v7x, 128 devices: a whole 4x4x4 slice. The times are simulated.
128 devices in a mesh: src: 32 (over x, y, core), tgt: 4 (over z).
Axes of the slice: x: 4, y: 4, z: 4, core: 2. Of those that a mesh axis runs over, the one named last changes fastest.
Arguments:
- source_embed: bfloat16 [65536, 768], P('src'), may hold values from -5 to 5
- target_embed: bfloat16 [8192, 768], P('tgt'), may hold values from -5 to 5
- source_potential: float32 [65536], P('src'), may hold values from -7 to -4
- target_potential: float32 [8192], replicated, may hold values from -5.5 to -3.5
- active_blocks: int32 [256, 24], P('src'), may hold values from 0 to 31, as said below
- active_count: int32 [256], P('src'), may hold values from 1 to 24, as said below
Outputs:
- grad_source: bfloat16 [65536, 768], P('src', 'tgt')
- grad_target: bfloat16 [8192, 768], P('tgt')
Inputs may be any that keep to these rules, and one draw needn't show every extreme that they name: `active_blocks`: each block's 24 entries are distinct target block ids; only the first active_count entries are used. Some source block lists all 24. `active_count`: counts differ strongly between source blocks and between devices of src; some block has exactly 24.
All inputs are finite; a program needn't handle non-finite values.
Results may differ from a plain program's by a relative error of at most 0.005.
Values may be sent and summed in bfloat16 or wider, within the bound.
A program may use at most 128 MiB of HBM per device.

v0:
```python
import math

import jax
import jax.numpy as jnp
from jax import lax
from jax.sharding import PartitionSpec as P

D = 768
BLOCK = 256


def shards(
    source_embed, target_embed, source_potential, target_potential, active_blocks, active_count
):
    rows_here = source_embed.shape[0]
    blocks_here = rows_here // BLOCK
    target_here = target_embed.shape[0]
    shard_blocks = target_here // BLOCK
    list_length = active_blocks.shape[1]
    column = lax.axis_index("tgt")
    tpot_local = lax.dynamic_slice_in_dim(target_potential, column * target_here, target_here, 0)
    block_ids = column * shard_blocks + jnp.arange(shard_blocks, dtype=jnp.int32)
    live = jnp.arange(list_length, dtype=jnp.int32)[None, :] < active_count[:, None]
    hits = (active_blocks[:, :, None] == block_ids[None, None, :]) & live[:, :, None]
    block_mask = jnp.any(hits, axis=1)
    scores = lax.dot_general(
        source_embed, target_embed, (((1,), (1,)), ((), ())), preferred_element_type=jnp.float32
    )
    scale = 2.0 / math.sqrt(D)
    expo = jnp.exp(source_potential[:, None] + tpot_local[None, :] + scores * scale)
    expo = expo.reshape(blocks_here, BLOCK, shard_blocks, BLOCK)
    plan = (
        jnp.where(block_mask[:, None, :, None], expo, 0.0)
        .astype(jnp.bfloat16)
        .reshape(rows_here, target_here)
    )
    source_part = jnp.dot(plan, target_embed, preferred_element_type=jnp.float32)
    target_part = lax.dot_general(
        plan, source_embed, (((0,), (0,)), ((), ())), preferred_element_type=jnp.float32
    )
    source_final = lax.psum_scatter(source_part, "tgt", scatter_dimension=1, tiled=True).astype(
        jnp.bfloat16
    )
    target_final = lax.psum(target_part, "src").astype(jnp.bfloat16)
    return (source_final, target_final)


def solution(mesh):
    return jax.shard_map(
        shards,
        mesh=mesh,
        in_specs=(P("src", None), P("tgt", None), P("src"), P(), P("src", None), P("src")),
        out_specs=(P("src", "tgt"), P("tgt", None)),
        check_vma=False,
    )
```

profile of v0, /device:TPU:32, one launch (start us, length us, event | category | flops | bytes accessed | tf_op | source)
XLA Modules:
  0.0 216.0 jit_solution(9706840131953591894)
XLA Ops:
  7.2 0.0 copy-start
  7.2 0.0 reduce-scatter.2.cloned.1.call-start
  7.2 0.9 iota_compare_fusion
  8.1 1.0 and_reduce_fusion
  9.1 0.0 copy-start.1
  9.1 1.1 broadcast_in_dim.10
  10.3 4.1 %copy.8 = pred[256,8,8,256]{3,1,2,0:T(8,128)(4,1)} copy(pred[256,8,8,256]{3,2,1,0:T(8,128)(4,1)S(1)} %bitcast.9) | data formatting | bytes 8388608
  14.4 0.7 dynamic_slice.3
  15.1 0.0 copy-done
  15.1 0.0 copy-done.1
  15.1 12.0 %select_convert_fusion = bf16[2048,2048]{1,0:T(8,128)(2,1)S(1)} fusion(pred[2048,2048]{1,0:T(8,128)(4,1)} %bitcast.10, f32[2048]{0:T(1024)S(1)} %dynamic_slice.3, f32[2048]{0:T(1024)S(1)} %copy-done.1, bf16[2048,768]{1,0:T(8,128)(2,1)} %param.6, bf16[2048,768]{1,0:T(8,128)(2,1)S(1)} %copy-done), kind=kOutput, calls=%fused_computation | convolution fusion | flops 6463422464 | bytes 18890752 | tf_op jit(solution)/shard_map/dot_general | solution.py:26
  27.1 0.0 copy-start.2
  27.1 3.2 %copy-done.2 = bf16[2048,2048]{1,0:T(8,128)(2,1)} copy-done((bf16[2048,2048]{1,0:T(8,128)(2,1)}, bf16[2048,2048]{1,0:T(8,128)(2,1)S(1)}, u32[]{:S(2)}) %copy-start.2) | copy-done | bytes 8388632
  30.3 8.7 %fusion = f32[2048,768]{0,1:T(8,128)} fusion(bf16[2048,2048]{1,0:T(8,128)(2,1)S(1)} %select_convert_fusion, bf16[2048,768]{1,0:T(8,128)(2,1)S(1)} %copy-done), kind=kOutput, calls=%fused_computation.4 | convolution fusion | flops 6442450944 | bytes 17825792 | tf_op jit(solution)/shard_map/dot_general | solution.py:37
  39.1 0.0 reduce-scatter.2.cloned.1.call-update
  39.1 12.3 %fusion.1 = f32[2048,768]{1,0:T(8,128)} fusion(bf16[2048,2048]{1,0:T(8,128)(2,1)} %copy-done.2, bf16[2048,768]{1,0:T(8,128)(2,1)} %param.6), kind=kOutput, calls=%fused_computation.5 | convolution fusion | flops 6442450944 | bytes 17825792 | tf_op jit(solution)/shard_map/dot_general | solution.py:38
  51.3 155.4 %all-reduce.1 = bf16[2048,768]{1,0:T(8,128)(2,1)} all-reduce(f32[2048,768]{1,0:T(8,128)} %fusion.1), channel_id=1, replica_groups=mesh['src'=32,'tgt'=4] {'src'}, use_global_device_ids=true, to_apply=%region_2.3 | all-reduce | flops 1572864 | bytes 9437184 | tf_op jit(solution)/shard_map/psum | solution.py:44
  206.7 0.0 reduce-scatter.2.cloned.1.call-done
  206.7 2.4 %convert_element_type.11 = bf16[2048,192]{0,1:T(8,128)(2,1)} convert(f32[2048,192]{0,1:T(8,128)} %reduce-scatter.2.cloned.1.call-done) | non-fusion elementwise | flops 393216 | bytes 2359296 | tf_op jit(solution)/shard_map/convert_element_type | solution.py:41
  (1 shorter events, 0.0 us)
Async XLA Ops:
  7.2 7.9 %copy-start = (bf16[2048,768]{1,0:T(8,128)(2,1)S(1)}, bf16[2048,768]{1,0:T(8,128)(2,1)}, u32[]{:S(2)}) copy-start(bf16[2048,768]{1,0:T(8,128)(2,1)} %param.7) | copy-start | bytes 9437188
  7.2 199.5 %reduce-scatter.2.cloned.1.call-start = ((), (), s32[]{:S(2)}) async-start(), calls=%async_computation.1 | async-start | bytes 7864320 | tf_op jit(solution)/shard_map/reduce_scatter | solution.py:41
  9.1 6.0 %copy-start.1 = (f32[2048]{0:T(1024)S(1)}, f32[2048]{0:T(1024)}, u32[]{:S(2)}) copy-start(f32[2048]{0:T(1024)} %param.8) | copy-start | bytes 24580
  27.1 3.2 %copy-start.2 = (bf16[2048,2048]{1,0:T(8,128)(2,1)}, bf16[2048,2048]{1,0:T(8,128)(2,1)S(1)}, u32[]{:S(2)}) copy-start(bf16[2048,2048]{1,0:T(8,128)(2,1)S(1)} %select_convert_fusion) | copy-start | bytes 25165828
Sparse Core Ops, SparseCore 0:
  39.2 64.7 reduce-scatter.1
where the time goes:
time: 216 us
  blocking collectives  155 us (72%)
  matrix products  33 us (15%)
  between operations  14.1 us (7%)
  local copies, waits for them, and re-layouts  9.16 us (4%)
  other arithmetic  4.26 us (2%)
    psum x1, blocking collectives, shards(): target_final = lax.psum(target_part, 'src').astype(jnp.bfloat16)  155 us
    dot_general x1, matrix products, shards(): lax.dot_general(plan, source_embed, (((0,), (0,)), ((), ())), preferred_e...  12.3 us
    dot_general x1, matrix products, shards(): lax.dot_general(source_embed, target_embed, (((1,), (1,)), ((), ())), pre...  12 us
    dot_general x1, matrix products, shards(): jnp.dot(plan, target_embed, preferred_element_type=jnp.float32)  8.74 us
    unnamed x7, local copies, waits for them, and re-layouts  7.32 us
  transfers between devices with their start and end apart: 1, of which 0 were waited for; matrix products, arithmetic and copies ran while one was open for 6% of the time, Pallas kernels for 0%

commit v1 on v0

v1 whole, which is shorter than its diff:
```python
import functools
import math

import jax
import jax.numpy as jnp
from jax import lax
from jax.experimental import pallas as pl
from jax.experimental.pallas import tpu as pltpu
from jax.sharding import PartitionSpec as P

D = 768
BLOCK = 256
ROWS = 2048
LOG2E = 1.4426950408889634
SCALE = 2.0 / math.sqrt(D) * LOG2E
MESH = pl.DeviceIdType.MESH
F32 = jnp.float32
BF16 = jnp.bfloat16


def kernel(
    s_hbm, t_hbm, sp_ref, tp_ref, ids_ref, cnt_ref, gs_out, gt_out,
    s_v, t_v, plan, bias,
    z_part, z_send, z_recv, z_out,
    t_part, c_send, c_recv, x_send, x_recv, y_part, y_send, y_recv, g_out,
    load_sem, zs, zr, zo, cs, cr, xs, xr, ys, yr, ags, agr, ls, ks, kr,
):
    src = lax.axis_index("src")
    z = lax.axis_index("tgt")
    x = src // 8
    y = (src // 2) % 4
    core = src % 2

    def at(x_, y_, core_, z_):
        return ((x_ * 4 + y_) * 2 + core_, z_)

    def along(path, step):
        if path == 0:
            return at((x + step) % 4, y, core, z)
        return at(x, (y + step) % 4, core, z)

    def along_z(step):
        return at(x, y, core, (z + step) % 4)

    other = at(x, y, 1 - core, z)
    peers = [along_z(1), along_z(3), other]
    peers += [along(p, d) for p in (0, 1) for d in (1, 2, 3)]

    barrier = pltpu.get_barrier_semaphore()
    for peer in peers:
        pl.semaphore_signal(barrier, inc=1, device_id=peer, device_id_type=MESH)

    t_load = pltpu.make_async_copy(t_hbm, t_v, load_sem.at[0])
    s0_load = pltpu.make_async_copy(
        s_hbm.at[pl.ds(0, 512)], s_v.at[pl.ds(0, 512)], load_sem.at[1]
    )
    s1_load = pltpu.make_async_copy(
        s_hbm.at[pl.ds(512, 1536)], s_v.at[pl.ds(512, 1536)], load_sem.at[2]
    )
    t_load.start()
    s0_load.start()
    s1_load.start()

    sub = lax.broadcasted_iota(jnp.int32, (8, 24), 0)
    lane = lax.broadcasted_iota(jnp.int32, (8, 24), 1)
    count = jnp.zeros((8, 24), jnp.int32)
    for a in range(8):
        count = jnp.where(sub == a, cnt_ref[a], count)
    ids = jnp.where(lane < count, ids_ref[...], -1)
    tp = tp_ref[pl.ds(pl.multiple_of(z * 16, 16), 16), :] * LOG2E
    for b in range(8):
        hit = jnp.max(jnp.where(ids == z * 8 + b, 1.0, 0.0), axis=1, keepdims=True)
        for h in range(2):
            row = tp[2 * b + h:2 * b + h + 1, :]
            bias[:, b * 256 + h * 128:b * 256 + (h + 1) * 128] = jnp.where(
                hit > 0.5, row, -1e30
            )

    def remote(src_ref, dst_ref, send, recv, dev):
        return pltpu.make_async_remote_copy(
            src_ref=src_ref, dst_ref=dst_ref, send_sem=send, recv_sem=recv,
            device_id=dev, device_id_type=MESH,
        )

    def score(first, blocks):
        rows = blocks * BLOCK
        base = pl.multiple_of(first * BLOCK, BLOCK)
        lhs = s_v[pl.ds(base, rows), :]
        pots = []
        for h in range(2 * blocks):
            row = sp_ref[pl.ds(first * 2 + h, 1), :] * LOG2E
            pots.append(jnp.transpose(jnp.broadcast_to(row, (128, 128))))
        for n in range(4):
            cols = slice(n * 512, (n + 1) * 512)
            s = lax.dot_general(
                lhs, t_v[cols, :], (((1,), (1,)), ((), ())), preferred_element_type=F32
            )
            for i in range(blocks):
                tpr = bias[pl.ds(first + i, 1), cols]
                for h in range(2):
                    q = 2 * i + h
                    part = s[q * 128:(q + 1) * 128, :]
                    pot = jnp.concatenate([pots[q]] * 4, axis=1)
                    e = jnp.exp2(part * SCALE + (pot + tpr))
                    plan[pl.ds(base + q * 128, 128), cols] = e.astype(BF16)

    def z_copy(a, m):
        return remote(
            z_send.at[a, m], z_recv.at[a, m], zs.at[a, m], zr.at[a, m],
            along_z(1 if m % 2 == 0 else 3),
        )

    lane_low = lax.broadcasted_iota(jnp.int32, (128, 128), 1) < 64

    def source_block(a):
        base = pl.multiple_of(a * BLOCK, BLOCK)
        g = jnp.dot(plan[pl.ds(base, BLOCK), :], t_v[...], preferred_element_type=F32)
        for o, tile in ((0, 0), (1, 2), (2, 3), (3, 5)):
            z_part[a, o, 0:256, :] = g[:, tile * 128:(tile + 1) * 128]
        for o, tile in ((0, 1), (2, 4)):
            top = g[0:128, tile * 128:(tile + 1) * 128]
            low = g[128:256, tile * 128:(tile + 1) * 128]
            z_part[a, o, 256:384, :] = jnp.where(lane_low, top, pltpu.roll(low, 64, 1))
            z_part[a, o + 1, 256:384, :] = jnp.where(lane_low, pltpu.roll(top, 64, 1), low)
        for m, (o, r) in enumerate(((2, 0), (2, 192), (1, 192), (3, 0))):
            z_send[a, m] = z_part[a, (z + o) % 4, r:r + 192, :].astype(BF16)
            z_copy(a, m).start()

    def z_second(a):
        for m, o, r in ((0, 1, 0), (1, 3, 192)):
            z_copy(a, m).wait_recv()
            total = z_part[a, (z + o) % 4, r:r + 192, :] + z_recv[a, m].astype(F32)
            z_send[a, 4 + m] = total.astype(BF16)
            z_copy(a, 4 + m).start()

    def z_out_copy(a):
        rows = pl.ds(pl.multiple_of(a * BLOCK, BLOCK), BLOCK)
        return pltpu.make_async_copy(z_out.at[rows], gs_out.at[rows], zo.at[a])

    def z_final(a):
        for m in (2, 3, 4, 5):
            z_copy(a, m).wait_recv()
        first = z_part[a, z, 0:192, :] + (
            z_recv[a, 4].astype(F32) + z_recv[a, 3].astype(F32)
        )
        second = z_part[a, z, 192:384, :] + (
            z_recv[a, 2].astype(F32) + z_recv[a, 5].astype(F32)
        )
        whole = jnp.concatenate([first, second], axis=0)
        packed = whole[256:384, :]
        rolled = pltpu.roll(packed, 64, 1)
        odd = (z % 2) == 1
        for h in range(2):
            full = whole[h * 128:(h + 1) * 128, :]
            half = packed if h == 0 else rolled
            turned = pltpu.roll(full, 64, 1)
            left = jnp.where(odd, jnp.where(lane_low, half, turned), full)
            right = jnp.where(odd, turned, half)
            rows = pl.ds(pl.multiple_of(a * BLOCK + h * 128, 128), 128)
            z_out[rows, 0:128] = left.astype(BF16)
            z_out[rows, 128:192] = right[:, 0:64].astype(BF16)
        z_out_copy(a).start()

    def c_copy(c):
        return remote(c_send.at[c], c_recv.at[c], cs.at[c], cr.at[c], other)

    def target_chunk(c):
        cols = pl.ds(pl.multiple_of(c * 512, 512), 512)
        g = lax.dot_general(
            plan[:, cols], s_v[...], (((0,), (0,)), ((), ())), preferred_element_type=F32
        )
        t_part[c, 0] = g[0:256, :]
        t_part[c, 1] = g[256:512, :]
        c_send[c] = t_part[c, 1 - core].astype(BF16)
        c_copy(c).start()

    def x_copy(c, p, m):
        return remote(
            x_send.at[c, p, m], x_recv.at[c, p, m], xs.at[c, p, m], xr.at[c, p, m],
            along(p, 1 if m % 2 == 0 else 3),
        )

    def first_of(p):
        return x if p == 0 else y

    def second_of(p):
        return y if p == 0 else x

    def cols_of(p):
        return slice(p * 384, (p + 1) * 384)

    def rows_at(start, size):
        return pl.ds(pl.multiple_of(start, 16), size)

    def x_first(c):
        c_copy(c).wait_recv()
        t_part[c, core] = t_part[c, core] + c_recv[c].astype(F32)
        for m, (o, r) in enumerate(((2, 0), (2, 32), (1, 32), (3, 0))):
            for p in range(2):
                piece = (first_of(p) + o) % 4
                x_send[c, p, m] = t_part[
                    c, core, rows_at(piece * 64 + r, 32), cols_of(p)
                ].astype(BF16)
                x_copy(c, p, m).start()

    def x_second(c):
        for m, o, r in ((0, 1, 0), (1, 3, 32)):
            for p in range(2):
                piece = (first_of(p) + o) % 4
                x_copy(c, p, m).wait_recv()
                total = t_part[
                    c, core, rows_at(piece * 64 + r, 32), cols_of(p)
                ] + x_recv[c, p, m].astype(F32)
                x_send[c, p, 4 + m] = total.astype(BF16)
                x_copy(c, p, 4 + m).start()

    def y_copy(c, p, d):
        piece = (second_of(p) + d) % 4
        return remote(
            y_send.at[c, p, rows_at(piece * 16, 16)], y_recv.at[c, p, d - 1],
            ys.at[c, p, d - 1], yr.at[c, p, d - 1], along(1 - p, d),
        )

    def x_third(c):
        for p in range(2):
            for m in (2, 3, 4, 5):
                x_copy(c, p, m).wait_recv()
            mine = first_of(p) * 64
            low = t_part[c, core, rows_at(mine, 32), cols_of(p)] + (
                x_recv[c, p, 4].astype(F32) + x_recv[c, p, 3].astype(F32)
            )
            high = t_part[c, core, rows_at(mine + 32, 32), cols_of(p)] + (
                x_recv[c, p, 2].astype(F32) + x_recv[c, p, 5].astype(F32)
            )
            y_part[c, p, 0:32, :] = low
            y_part[c, p, 32:64, :] = high
            y_send[c, p, 0:32, :] = low.astype(BF16)
            y_send[c, p, 32:64, :] = high.astype(BF16)
            for d in (1, 2, 3):
                y_copy(c, p, d).start()

    def y_gather(c, p, d):
        rows = rows_at(first_of(p) * 64 + second_of(p) * 16, 16)
        piece = g_out.at[c, rows, cols_of(p)]
        return remote(piece, piece, ys.at[c, p, 2 + d], yr.at[c, p, 2 + d], along(1 - p, d))

    def y_final(c):
        for p in range(2):
            for d in (1, 2, 3):
                y_copy(c, p, d).wait_recv()
            mine = y_part[c, p, rows_at(second_of(p) * 16, 16), :]
            total = mine + (
                y_recv[c, p, 0].astype(F32)
                + y_recv[c, p, 1].astype(F32)
                + y_recv[c, p, 2].astype(F32)
            )
            rows = rows_at(first_of(p) * 64 + second_of(p) * 16, 16)
            g_out[c, rows, cols_of(p)] = total.astype(BF16)
            for d in (1, 2, 3):
                y_gather(c, p, d).start()

    def a_copy(c, p, m):
        start = first_of(p) * 64
        size = 64
        if m == 2:
            start, size = ((first_of(p) + 3) % 4) * 64, 32
        if m == 3:
            start, size = ((first_of(p) + 1) % 4) * 64 + 32, 32
        piece = g_out.at[c, rows_at(start, size), cols_of(p)]
        return remote(
            piece, piece, ags.at[c, p, m], agr.at[c, p, m], along(p, 1 if m % 2 == 0 else 3)
        )

    def gather_first(c):
        for p in range(2):
            for d in (1, 2, 3):
                y_gather(c, p, d).wait_recv()
            for m in (0, 1):
                a_copy(c, p, m).start()

    def gather_second(c):
        for m in (0, 1):
            for p in range(2):
                a_copy(c, p, m).wait_recv()
                a_copy(c, p, 2 + m).start()

    def out_rows(c):
        return pl.ds(pl.multiple_of(c * 512 + core * 256, 256), 256)

    def l_copy(c):
        return pltpu.make_async_copy(g_out.at[c], gt_out.at[out_rows(c)], ls.at[c])

    def k_copy(c):
        return remote(g_out.at[c], gt_out.at[out_rows(c)], ks.at[c], kr.at[c], other)

    def gather_final(c):
        for m in (2, 3):
            for p in range(2):
                a_copy(c, p, m).wait_recv()
        k_copy(c).start()
        l_copy(c).start()

    t_load.wait()
    s0_load.wait()
    score(0, 1)
    pl.semaphore_wait(barrier, len(peers))

    @pl.loop(0, 2)
    def _(a):
        source_block(a)

        @pl.when(a == 0)
        def _():
            score(1, 1)

    s1_load.wait()

    @pl.loop(1, 4)
    def _(d):
        score(d * 2, 2)

        @pl.when(d >= 2)
        def _():
            z_second(d - 2)

    def when(cond, fn, arg):
        @pl.when(cond)
        def _():
            fn(arg)

    @pl.loop(0, 11)
    def _(i):
        when(i < 6, source_block, i + 2)
        when((i >= 1) & (i < 5), x_first, i - 1)
        when(i < 4, target_chunk, i)
        when((i >= 1) & (i < 5), x_second, i - 1)
        when((i >= 2) & (i < 6), x_third, i - 2)
        when((i >= 3) & (i < 7), y_final, i - 3)
        when((i >= 4) & (i < 8), gather_first, i - 4)
        when((i >= 5) & (i < 9), gather_second, i - 5)
        when((i >= 6) & (i < 10), gather_final, i - 6)
        second = jnp.where(i < 5, i + 1, i - 2)
        when(((i >= 1) & (i < 5)) | ((i >= 8) & (i < 10)), z_second, second)
        when((i >= 1) & (i < 7), z_final, i - 1)

    z_final(6)
    z_final(7)

    @pl.loop(0, 4)
    def _(c):
        k_copy(c).wait()
        l_copy(c).wait()
        c_copy(c).wait_send()
        for p in range(2):
            for m in range(6):
                x_copy(c, p, m).wait_send()
            for d in (1, 2, 3):
                y_copy(c, p, d).wait_send()
                y_gather(c, p, d).wait_send()
            for m in range(4):
                a_copy(c, p, m).wait_send()

    @pl.loop(0, 8)
    def _(a):
        for m in range(6):
            z_copy(a, m).wait_send()
        z_out_copy(a).wait()


def shards(
    source_embed, target_embed, source_potential, target_potential, active_blocks, active_count
):
    vmem = pl.BlockSpec(memory_space=pltpu.VMEM)
    smem = pl.BlockSpec(memory_space=pltpu.SMEM)
    hbm = pl.BlockSpec(memory_space=pl.ANY)
    dma = pltpu.SemaphoreType.DMA
    return pl.pallas_call(
        kernel,
        out_shape=(
            jax.ShapeDtypeStruct((ROWS, D // 4), BF16),
            jax.ShapeDtypeStruct((ROWS, D), BF16),
        ),
        in_specs=[hbm, hbm, vmem, vmem, vmem, smem],
        out_specs=(hbm, hbm),
        scratch_shapes=[
            pltpu.VMEM((ROWS, D), BF16),
            pltpu.VMEM((ROWS, D), BF16),
            pltpu.VMEM((ROWS, ROWS), BF16),
            pltpu.VMEM((8, ROWS), F32),
            pltpu.VMEM((8, 4, 384, 128), F32),
            pltpu.VMEM((8, 6, 192, 128), BF16),
            pltpu.VMEM((8, 6, 192, 128), BF16),
            pltpu.VMEM((ROWS, D // 4), BF16),
            pltpu.VMEM((4, 2, 256, D), F32),
            pltpu.VMEM((4, 256, D), BF16),
            pltpu.VMEM((4, 256, D), BF16),
            pltpu.VMEM((4, 2, 6, 32, 384), BF16),
            pltpu.VMEM((4, 2, 6, 32, 384), BF16),
            pltpu.VMEM((4, 2, 64, 384), F32),
            pltpu.VMEM((4, 2, 64, 384), BF16),
            pltpu.VMEM((4, 2, 3, 16, 384), BF16),
            pltpu.VMEM((4, 256, D), BF16),
            dma((3,)),
            dma((8, 6)),
            dma((8, 6)),
            dma((8,)),
            dma((4,)),
            dma((4,)),
            dma((4, 2, 6)),
            dma((4, 2, 6)),
            dma((4, 2, 6)),
            dma((4, 2, 6)),
            dma((4, 2, 4)),
            dma((4, 2, 4)),
            dma((4,)),
            dma((4,)),
            dma((4,)),
        ],
        compiler_params=pltpu.CompilerParams(
            collective_id=0, has_side_effects=True, vmem_limit_bytes=56 * 2**20
        ),
        cost_estimate=pl.CostEstimate(
            flops=3 * 2 * ROWS * ROWS * D, bytes_accessed=12 * 2**20, transcendentals=ROWS * ROWS
        ),
    )(
        source_embed,
        target_embed,
        source_potential.reshape(16, 128),
        target_potential.reshape(64, 128),
        active_blocks,
        active_count,
    )


def solution(mesh):
    return jax.shard_map(
        shards,
        mesh=mesh,
        in_specs=(P("src", None), P("tgt", None), P("src"), P(), P("src", None), P("src")),
        out_specs=(P("src", "tgt"), P("tgt", None)),
        check_vma=False,
    )
```

time: 216 us -> 73.5 us (0.34)
  the two profiles are of different devices: /device:TPU:32 before, /device:TPU:0 now
where the time goes in v1:
time: 73.5 us; the launch traced here: 73.3 us
  Pallas kernels  66.7 us (91%)
  local copies, waits for them, and re-layouts  5.94 us (8%)
    pallas_call x1, Pallas kernels, shards(): pl.pallas_call(kernel, out_shape=(jax.ShapeDtypeStruct((ROWS, D // 4), BF...  66.7 us
    unnamed x1, local copies, waits for them, and re-layouts  3.75 us
    pallas_call x1, local copies, waits for them, and re-layouts, shards(): pl.pallas_call(kernel, out_shape=(jax.ShapeDtypeStruct((ROWS, D // 4), BF...  2.19 us

profile of v1, /device:TPU:0, one launch (start us, length us, event | category | flops | bytes accessed | tf_op | source)
XLA Modules:
  0.0 73.3 jit_solution(17586939169939947049)
XLA Ops:
  0.6 66.7 %shard_map.77 = (bf16[2048,192]{1,0:T(8,128)(2,1)}, bf16[2048,768]{1,0:T(8,128)(2,1)}) custom-call(bf16[2048,768]{1,0:T(8,128)(2,1)} %s_hbm.1, bf16[2048,768]{1,0:T(8,128)(2,1)} %t_hbm.1, f32[16,128]{1,0:T(8,128)} %bitcast.3, f32[64,128]{1,0:T(8,128)} %bitcast.2, s32[8,24]{1,0:T(8,128)} %ids_ref.1, s32[8]{0:T(128)} %cnt_ref.1), custom_call_target="tpu_custom_call" | custom-call | flops 19327352832 | bytes 12582912 | tf_op jit(solution)/shard_map/pallas_call | solution.py:377
  67.3 2.2 %copy.8 = bf16[2048,192]{0,1:T(8,128)(2,1)} copy(bf16[2048,192]{1,0:T(8,128)(2,1)} %get-tuple-element.2) | data formatting | bytes 1572864 | tf_op jit(solution)/shard_map/pallas_call | solution.py:377
  69.5 3.8 %copy.10 = bf16[2048,768]{1,0:T(8,128)(2,1)} copy(bf16[2048,768]{1,0:T(8,128)(2,1)} %get-tuple-element.7) | data formatting | bytes 6291456

commit v2 on v1

v2 whole, which is shorter than its diff:
```python
import functools
import math

import jax
import jax.numpy as jnp
from jax import lax
from jax.experimental import pallas as pl
from jax.experimental.pallas import tpu as pltpu
from jax.sharding import PartitionSpec as P

D = 768
BLOCK = 256
ROWS = 2048
LOG2E = 1.4426950408889634
SCALE = 2.0 / math.sqrt(D) * LOG2E
MESH = pl.DeviceIdType.MESH
F32 = jnp.float32
BF16 = jnp.bfloat16

SCHEDULE = (
    ("S00", "S01", "S02", "S03", "G0",),
    ("G1",),
    ("S10",),
    ("S11",),
    ("S12",),
    ("S13",),
    ("S20", "S30",),
    ("T0",),
    ("S21", "S31",),
    ("B0",),
    ("X0",),
    ("T1",),
    ("B1",),
    ("G2",),
    ("X1",),
    ("S22", "S32",),
    ("T2",),
    ("Y0",),
    ("G3",),
    ("X2",),
    ("S23", "S33",),
    ("T3",),
    ("Y1",),
    ("F0",),
    ("B2",),
    ("G4",),
    ("X3",),
    ("B3",),
    ("G5",),
    ("Y2",),
    ("F1",),
    ("H0",),
    ("G6",),
    ("G7",),
    ("B4",),
    ("F2",),
    ("Y3",),
    ("H1",),
    ("I0",),
    ("B5",),
    ("C0",),
    ("F3",),
    ("H2",),
    ("B6",),
    ("C1",),
    ("B7",),
    ("C2",),
    ("I1",),
    ("C3",),
    ("H3",),
    ("I2",),
    ("C4",),
    ("C5",),
    ("C6",),
    ("I3",),
    ("C7",),
)


def kernel(
    s_hbm, t_hbm, sp_ref, tp_ref, ids_ref, cnt_ref, gs_out, gt_out,
    s_v, t_v, plan, bias,
    z_part, z_send, z_recv, z2_send, z2_recv, z_out,
    t_part, c_send, c_recv, x_send, x_recv, y_part, y_send, y_recv, g_out,
    load_sem, zs, zr, zo, cs, cr, xs, xr, ys, yr, ags, agr, ls, ks, kr,
):
    src = lax.axis_index("src")
    z = lax.axis_index("tgt")
    x = src // 8
    y = (src // 2) % 4
    core = src % 2

    def at(x_, y_, core_, z_):
        return ((x_ * 4 + y_) * 2 + core_, z_)

    def along(path, step):
        if path == 0:
            return at((x + step) % 4, y, core, z)
        return at(x, (y + step) % 4, core, z)

    def along_z(step):
        return at(x, y, core, (z + step) % 4)

    other = at(x, y, 1 - core, z)
    peers = [along_z(1), along_z(3), other]
    peers += [along(p, d) for p in (0, 1) for d in (1, 2, 3)]

    barrier = pltpu.get_barrier_semaphore()
    for peer in peers:
        pl.semaphore_signal(barrier, inc=1, device_id=peer, device_id_type=MESH)

    def load(n, hbm_ref, ref, start, size):
        rows = pl.ds(start, size)
        return pltpu.make_async_copy(hbm_ref.at[rows], ref.at[rows], load_sem.at[n])

    loads = [load(0, s_hbm, s_v, 0, 512)]
    loads += [load(1 + n, t_hbm, t_v, n * 512, 512) for n in range(4)]
    loads += [load(5, s_hbm, s_v, 512, 1536)]
    for copy in loads:
        copy.start()

    sub = lax.broadcasted_iota(jnp.int32, (8, 24), 0)
    lane = lax.broadcasted_iota(jnp.int32, (8, 24), 1)
    count = jnp.zeros((8, 24), jnp.int32)
    for a in range(8):
        count = jnp.where(sub == a, cnt_ref[a], count)
    ids = jnp.where(lane < count, ids_ref[...], -1)
    tp = tp_ref[pl.ds(pl.multiple_of(z * 16, 16), 16), :] * LOG2E
    for b in range(8):
        hit = jnp.max(jnp.where(ids == z * 8 + b, 1.0, 0.0), axis=1, keepdims=True)
        for h in range(2):
            row = tp[2 * b + h:2 * b + h + 1, :]
            bias[:, b * 256 + h * 128:b * 256 + (h + 1) * 128] = jnp.where(
                hit > 0.5, row, -1e30
            )

    def remote(src_ref, dst_ref, send, recv, dev):
        return pltpu.make_async_remote_copy(
            src_ref=src_ref, dst_ref=dst_ref, send_sem=send, recv_sem=recv,
            device_id=dev, device_id_type=MESH,
        )

    def score(first, blocks, n):
        rows = blocks * BLOCK
        base = first * BLOCK
        cols = slice(n * 512, (n + 1) * 512)
        s = lax.dot_general(
            s_v[base:base + rows, :], t_v[cols, :], (((1,), (1,)), ((), ())),
            preferred_element_type=F32,
        )
        for i in range(blocks):
            tpr = bias[first + i:first + i + 1, cols]
            for h in range(2):
                q = 2 * i + h
                row = sp_ref[first * 2 + q:first * 2 + q + 1, :] * LOG2E
                pot = jnp.transpose(jnp.broadcast_to(row, (128, 128)))
                pot = jnp.concatenate([pot] * 4, axis=1)
                e = jnp.exp2(s[q * 128:(q + 1) * 128, :] * SCALE + (pot + tpr))
                plan[base + q * 128:base + (q + 1) * 128, cols] = e.astype(BF16)

    def z_copy(a, m):
        first, way = m < 2, m % 2
        return remote(
            z_send.at[a, way] if first else z2_send.at[a, way],
            z_recv.at[a, way] if first else z2_recv.at[a, way],
            zs.at[a, m], zr.at[a, m], along_z(1 if way == 0 else 3),
        )

    lane_low = lax.broadcasted_iota(jnp.int32, (128, 128), 1) < 64

    def source_body(first, blocks):
        base = first * BLOCK
        whole = jnp.dot(
            plan[base:base + blocks * BLOCK, :], t_v[...], preferred_element_type=F32
        )
        for i in range(blocks):
            a = first + i
            g = whole[i * BLOCK:(i + 1) * BLOCK, :]
            for o, tile in ((0, 0), (1, 2), (2, 3), (3, 5)):
                z_part[a, o, 0:256, :] = g[:, tile * 128:(tile + 1) * 128]
            for o, tile in ((0, 1), (2, 4)):
                top = g[0:128, tile * 128:(tile + 1) * 128]
                low = g[128:256, tile * 128:(tile + 1) * 128]
                z_part[a, o, 256:384, :] = jnp.where(lane_low, top, pltpu.roll(low, 64, 1))
                z_part[a, o + 1, 256:384, :] = jnp.where(lane_low, pltpu.roll(top, 64, 1), low)
            for way, half, o, r in ((0, 0, 2, 0), (0, 1, 1, 192), (1, 0, 2, 192), (1, 1, 3, 0)):
                z_send[a, way, half * 192:half * 192 + 192, :] = z_part[
                    a, (z + o) % 4, r:r + 192, :
                ].astype(BF16)

    def pair_start(pair):
        source_start(2 * pair)
        source_start(2 * pair + 1)

    def source_start(a):
        for m in (0, 1):
            z_copy(a, m).start()

    def second_wait(a):
        for m in (0, 1):
            z_copy(a, m).wait_recv()

    def second_body(a):
        for way, o, r in ((0, 1, 0), (1, 3, 192)):
            total = z_part[a, (z + o) % 4, r:r + 192, :] + z_recv[a, way, 0:192, :].astype(F32)
            z2_send[a, way] = total.astype(BF16)

    def second_start(a):
        for m in (2, 3):
            z_copy(a, m).start()

    def z_out_copy(a):
        cols = pl.ds(pl.multiple_of(a * BLOCK, BLOCK), BLOCK)
        return pltpu.make_async_copy(z_out.at[:, cols], gs_out.at[:, cols], zo.at[a])

    def final_wait(a):
        for m in (2, 3):
            z_copy(a, m).wait_recv()

    def final_body(a):
        first = z_part[a, z, 0:192, :] + (
            z2_recv[a, 0].astype(F32) + z_recv[a, 1, 192:384, :].astype(F32)
        )
        second = z_part[a, z, 192:384, :] + (
            z_recv[a, 0, 192:384, :].astype(F32) + z2_recv[a, 1].astype(F32)
        )
        whole = jnp.concatenate([first, second], axis=0)
        packed = whole[256:384, :]
        rolled = pltpu.roll(packed, 64, 1)
        odd = (z % 2) == 1
        for h in range(2):
            full = whole[h * 128:(h + 1) * 128, :]
            half = packed if h == 0 else rolled
            turned = pltpu.roll(full, 64, 1)
            left = jnp.where(odd, jnp.where(lane_low, half, turned), full)
            right = jnp.where(odd, turned, half)
            cols = pl.ds(pl.multiple_of(a * BLOCK + h * 128, 128), 128)
            z_out[0:128, cols] = jnp.transpose(left).astype(BF16)
            z_out[128:192, cols] = jnp.transpose(right)[0:64, :].astype(BF16)

    def final_start(a):
        z_out_copy(a).start()
        for m in range(4):
            z_copy(a, m).wait_send()

    def c_copy(c):
        return remote(c_send.at[c], c_recv.at[c], cs.at[c], cr.at[c], other)

    def target_body(c):
        cols = slice(c * 512, (c + 1) * 512)
        g = lax.dot_general(
            plan[:, cols], s_v[...], (((0,), (0,)), ((), ())), preferred_element_type=F32
        )
        low, high = g[0:256, :], g[256:512, :]
        t_part[c] = jnp.where(core == 0, low, high)
        c_send[c] = jnp.where(core == 0, high, low).astype(BF16)

    def target_start(c):
        c_copy(c).start()

    def x_copy(c, p, d):
        return remote(
            x_send.at[c, p, d - 1], x_recv.at[c, p, d - 1],
            xs.at[c, p, d - 1], xr.at[c, p, d - 1], along(p, d),
        )

    def first_of(p):
        return x if p == 0 else y

    def second_of(p):
        return y if p == 0 else x

    def cols_of(p):
        return slice(p * 384, (p + 1) * 384)

    def rows_at(start, size):
        return pl.ds(pl.multiple_of(start, 16), size)

    def x_wait(c):
        c_copy(c).wait_recv()

    def x_body(c):
        t_part[c] = t_part[c] + c_recv[c].astype(F32)
        for d in (1, 2, 3):
            for p in range(2):
                piece = (first_of(p) + d) % 4
                x_send[c, p, d - 1] = t_part[
                    c, rows_at(piece * 64, 64), cols_of(p)
                ].astype(BF16)

    def x_start(c):
        for d in (2, 1, 3):
            for p in range(2):
                x_copy(c, p, d).start()

    def y_copy(c, p, d):
        piece = (second_of(p) + d) % 4
        return remote(
            y_send.at[c, p, rows_at(piece * 16, 16)], y_recv.at[c, p, d - 1],
            ys.at[c, p, d - 1], yr.at[c, p, d - 1], along(1 - p, d),
        )

    def y_wait(c):
        for p in range(2):
            for d in (1, 3, 2):
                x_copy(c, p, d).wait_recv()

    def y_body(c):
        for p in range(2):
            total = t_part[c, rows_at(first_of(p) * 64, 64), cols_of(p)] + (
                x_recv[c, p, 0].astype(F32)
                + x_recv[c, p, 1].astype(F32)
                + x_recv[c, p, 2].astype(F32)
            )
            y_part[c, p] = total
            y_send[c, p] = total.astype(BF16)

    def y_start(c):
        for d in (2, 1, 3):
            for p in range(2):
                y_copy(c, p, d).start()
        c_copy(c).wait_send()
        for p in range(2):
            for d in (1, 2, 3):
                x_copy(c, p, d).wait_send()

    def y_gather(c, p, d):
        rows = rows_at(first_of(p) * 64 + second_of(p) * 16, 16)
        piece = g_out.at[c, rows, cols_of(p)]
        return remote(piece, piece, ys.at[c, p, 2 + d], yr.at[c, p, 2 + d], along(1 - p, d))

    def f_wait(c):
        for p in range(2):
            for d in (1, 2, 3):
                y_copy(c, p, d).wait_recv()

    def f_body(c):
        for p in range(2):
            mine = y_part[c, p, rows_at(second_of(p) * 16, 16), :]
            total = mine + (
                y_recv[c, p, 0].astype(F32)
                + y_recv[c, p, 1].astype(F32)
                + y_recv[c, p, 2].astype(F32)
            )
            rows = rows_at(first_of(p) * 64 + second_of(p) * 16, 16)
            g_out[c, rows, cols_of(p)] = total.astype(BF16)

    def f_start(c):
        for d in (2, 1, 3):
            for p in range(2):
                y_gather(c, p, d).start()
        for p in range(2):
            for d in (1, 2, 3):
                y_copy(c, p, d).wait_send()

    def a_copy(c, p, d):
        piece = g_out.at[c, rows_at(first_of(p) * 64, 64), cols_of(p)]
        return remote(
            piece, piece, ags.at[c, p, d - 1], agr.at[c, p, d - 1], along(p, d)
        )

    def out_rows(c):
        return pl.ds(pl.multiple_of(c * 512 + core * 256, 256), 256)

    def k_copy(c):
        return remote(g_out.at[c], gt_out.at[out_rows(c)], ks.at[c], kr.at[c], other)

    def l_copy(c):
        return pltpu.make_async_copy(g_out.at[c], gt_out.at[out_rows(c)], ls.at[c])

    def h_wait(c):
        for p in range(2):
            for d in (1, 2, 3):
                y_gather(c, p, d).wait_recv()

    def h_start(c):
        for d in (2, 1, 3):
            for p in range(2):
                a_copy(c, p, d).start()
        for p in range(2):
            for d in (1, 2, 3):
                y_gather(c, p, d).wait_send()

    def i_start(c):
        for p in range(2):
            for d in (1, 3, 2):
                a_copy(c, p, d).wait_recv()
        k_copy(c).start()
        l_copy(c).start()
        for p in range(2):
            for d in (1, 2, 3):
                a_copy(c, p, d).wait_send()

    def close(c):
        k_copy(c).wait()
        l_copy(c).wait()

    def nothing(_):
        pass

    ops = {
        "S": (nothing, None, nothing),
        "G": (nothing, lambda a: source_body(a, 1), source_start),
        "P": (nothing, lambda pair: source_body(2 * pair, 2), pair_start),
        "B": (second_wait, second_body, second_start),
        "C": (final_wait, final_body, final_start),
        "T": (nothing, target_body, target_start),
        "X": (x_wait, x_body, x_start),
        "Y": (y_wait, y_body, y_start),
        "F": (f_wait, f_body, f_start),
        "H": (h_wait, nothing, h_start),
        "I": (nothing, nothing, i_start),
    }
    for copy in loads[:5]:
        copy.wait()
    for index, block in enumerate(SCHEDULE):
        if index == 2:
            loads[5].wait()
        for op in block:
            ops[op[0]][0](int(op[1]))
        for op in block:
            if op[0] == "S":
                score(int(op[1]) * 2, 2, int(op[2]))
            else:
                ops[op[0]][1](int(op[1]))
        if index == 0:
            pl.semaphore_wait(barrier, len(peers))
        for op in block:
            ops[op[0]][2](int(op[1]))

    for c in range(4):
        close(c)
    for a in range(8):
        z_out_copy(a).wait()


def shards(
    source_embed, target_embed, source_potential, target_potential, active_blocks, active_count
):
    vmem = pl.BlockSpec(memory_space=pltpu.VMEM)
    smem = pl.BlockSpec(memory_space=pltpu.SMEM)
    hbm = pl.BlockSpec(memory_space=pl.ANY)
    dma = pltpu.SemaphoreType.DMA
    source_t, target = pl.pallas_call(
        kernel,
        out_shape=(
            jax.ShapeDtypeStruct((D // 4, ROWS), BF16),
            jax.ShapeDtypeStruct((ROWS, D), BF16),
        ),
        in_specs=[hbm, hbm, vmem, vmem, vmem, smem],
        out_specs=(hbm, hbm),
        scratch_shapes=[
            pltpu.VMEM((ROWS, D), BF16),
            pltpu.VMEM((ROWS, D), BF16),
            pltpu.VMEM((ROWS, ROWS), BF16),
            pltpu.VMEM((8, ROWS), F32),
            pltpu.VMEM((8, 4, 384, 128), F32),
            pltpu.VMEM((8, 2, 384, 128), BF16),
            pltpu.VMEM((8, 2, 384, 128), BF16),
            pltpu.VMEM((8, 2, 192, 128), BF16),
            pltpu.VMEM((8, 2, 192, 128), BF16),
            pltpu.VMEM((D // 4, ROWS), BF16),
            pltpu.VMEM((4, 256, D), F32),
            pltpu.VMEM((4, 256, D), BF16),
            pltpu.VMEM((4, 256, D), BF16),
            pltpu.VMEM((4, 2, 3, 64, 384), BF16),
            pltpu.VMEM((4, 2, 3, 64, 384), BF16),
            pltpu.VMEM((4, 2, 64, 384), F32),
            pltpu.VMEM((4, 2, 64, 384), BF16),
            pltpu.VMEM((4, 2, 3, 16, 384), BF16),
            pltpu.VMEM((4, 256, D), BF16),
            dma((6,)),
            dma((8, 4)),
            dma((8, 4)),
            dma((8,)),
            dma((4,)),
            dma((4,)),
            dma((4, 2, 3)),
            dma((4, 2, 3)),
            dma((4, 2, 6)),
            dma((4, 2, 6)),
            dma((4, 2, 3)),
            dma((4, 2, 3)),
            dma((4,)),
            dma((4,)),
            dma((4,)),
        ],
        compiler_params=pltpu.CompilerParams(
            collective_id=0, has_side_effects=True, vmem_limit_bytes=56 * 2**20
        ),
        cost_estimate=pl.CostEstimate(
            flops=3 * 2 * ROWS * ROWS * D, bytes_accessed=12 * 2**20, transcendentals=ROWS * ROWS
        ),
    )(
        source_embed,
        target_embed,
        source_potential.reshape(16, 128),
        target_potential.reshape(64, 128),
        active_blocks,
        active_count,
    )
    return source_t.T, target


def solution(mesh):
    return jax.shard_map(
        shards,
        mesh=mesh,
        in_specs=(P("src", None), P("tgt", None), P("src"), P(), P("src", None), P("src")),
        out_specs=(P("src", "tgt"), P("tgt", None)),
        check_vma=False,
    )
```

time: 73.5 us -> 61.8 us (0.84)
  the two profiles are of different devices: /device:TPU:0 before, /device:TPU:1 now
where the time goes in v2:
time: 61.8 us; the launch traced here: 61.5 us
  Pallas kernels  55 us (89%)
  local copies, waits for them, and re-layouts  5.84 us (9%)
  between operations  0.64 us (1%)
    pallas_call x1, Pallas kernels, shards(): pl.pallas_call(kernel, out_shape=(jax.ShapeDtypeStruct((D // 4, ROWS), BF...  55 us
    unnamed x2, local copies, waits for them, and re-layouts  5.84 us

profile of v2, /device:TPU:1, one launch (start us, length us, event | category | flops | bytes accessed | tf_op | source)
XLA Modules:
  0.0 61.5 jit_solution(1527249052765855412)
XLA Ops:
  0.6 55.0 %shard_map.77 = (bf16[192,2048]{1,0:T(8,128)(2,1)}, bf16[2048,768]{1,0:T(8,128)(2,1)}) custom-call(bf16[2048,768]{1,0:T(8,128)(2,1)} %s_hbm.1, bf16[2048,768]{1,0:T(8,128)(2,1)} %t_hbm.1, f32[16,128]{1,0:T(8,128)} %bitcast.5, f32[64,128]{1,0:T(8,128)} %bitcast.4, s32[8,24]{1,0:T(8,128)} %ids_ref.1, s32[8]{0:T(128)} %cnt_ref.1), custom_call_target="tpu_custom_call" | custom-call | flops 19327352832 | bytes 12582912 | tf_op jit(solution)/shard_map/pallas_call | solution.py:444
  55.6 2.1 %copy.10 = bf16[2048,192]{0,1:T(8,128)(2,1)} copy(bf16[2048,192]{0,1:T(8,128)(2,1)} %bitcast.3) | data formatting | bytes 1572864
  57.7 3.8 %copy.11 = bf16[2048,768]{1,0:T(8,128)(2,1)} copy(bf16[2048,768]{1,0:T(8,128)(2,1)} %get-tuple-element.9) | data formatting | bytes 6291456

commit v3 on v2

--- a/solution.py
+++ b/solution.py
@@ -432,6 +432,25 @@
         close(c)
     for a in range(8):
         z_out_copy(a).wait()
+
+
+def finish(gs_in, gt_in, gs_out, gt_out, gs_v, gt_v, in_sem, out_sem):
+    pieces = []
+    for n in range(8):
+        rows = pl.ds(n * 256, 256)
+        pieces.append((gt_in.at[rows], gt_v.at[rows], gt_out.at[rows]))
+    for n in range(2):
+        rows = pl.ds(n * 96, 96)
+        pieces.append((gs_in.at[rows], gs_v.at[rows], gs_out.at[rows]))
+    reads = [pltpu.make_async_copy(a, b, in_sem.at[n]) for n, (a, b, _) in enumerate(pieces)]
+    writes = [pltpu.make_async_copy(b, c, out_sem.at[n]) for n, (_, b, c) in enumerate(pieces)]
+    for copy in reads:
+        copy.start()
+    for read, write in zip(reads, writes):
+        read.wait()
+        write.start()
+    for copy in writes:
+        copy.wait()
 
 
 def shards(
@@ -499,6 +518,22 @@
         active_blocks,
         active_count,
     )
+    source_t, target = pl.pallas_call(
+        finish,
+        out_shape=(
+            jax.ShapeDtypeStruct((D // 4, ROWS), BF16),
+            jax.ShapeDtypeStruct((ROWS, D), BF16),
+        ),
+        in_specs=[hbm, hbm],
+        out_specs=(hbm, hbm),
+        scratch_shapes=[
+            pltpu.VMEM((D // 4, ROWS), BF16),
+            pltpu.VMEM((ROWS, D), BF16),
+            dma((10,)),
+            dma((10,)),
+        ],
+        compiler_params=pltpu.CompilerParams(vmem_limit_bytes=56 * 2**20),
+    )(source_t, target)
     return source_t.T, target
 
 

time: 61.8 us -> 59.4 us (0.961)
  local copies, waits for them, and re-layouts: 5.84 us -> 0 us
  Pallas kernels: 55 us -> 58.4 us
    unnamed x2 -> x0, local copies, waits for them, and re-layouts: 5.84 us -> none
    pallas_call x0 -> x1, Pallas kernels: none -> 3.41 us  [shards(): pl.pallas_call(finish, out_shape=(jax.ShapeDtypeStruct((D // 4, ROWS), BF...]
where the time goes in v3:
time: 59.4 us; the launch traced here: 59.2 us
  Pallas kernels  58.4 us (98%)
  between operations  0.8 us (1%)
    pallas_call x1, Pallas kernels, shards(): pl.pallas_call(kernel, out_shape=(jax.ShapeDtypeStruct((D // 4, ROWS), BF...  55 us
    pallas_call x1, Pallas kernels, shards(): pl.pallas_call(finish, out_shape=(jax.ShapeDtypeStruct((D // 4, ROWS), BF...  3.41 us

profile of v3, /device:TPU:1, one launch (start us, length us, event | category | flops | bytes accessed | tf_op | source)
XLA Modules:
  0.0 59.2 jit_solution(15422472605149008865)
XLA Ops:
  0.6 55.0 %shard_map.77 = (bf16[192,2048]{1,0:T(8,128)(2,1)}, bf16[2048,768]{1,0:T(8,128)(2,1)}) custom-call(bf16[2048,768]{1,0:T(8,128)(2,1)} %s_hbm.1, bf16[2048,768]{1,0:T(8,128)(2,1)} %t_hbm.1, f32[16,128]{1,0:T(8,128)} %bitcast.5, f32[64,128]{1,0:T(8,128)} %bitcast.4, s32[8,24]{1,0:T(8,128)} %ids_ref.1, s32[8]{0:T(128)} %cnt_ref.1), custom_call_target="tpu_custom_call" | custom-call | flops 19327352832 | bytes 12582912 | tf_op jit(solution)/shard_map/pallas_call | solution.py:463
  55.6 3.4 %shard_map.78 = (bf16[192,2048]{1,0:T(8,128)(2,1)}, bf16[2048,768]{1,0:T(8,128)(2,1)}) custom-call(bf16[192,2048]{1,0:T(8,128)(2,1)} %get-tuple-element.6.gs_in, bf16[2048,768]{1,0:T(8,128)(2,1)} %get-tuple-element.7.gt_in), custom_call_target="tpu_custom_call" | custom-call | tf_op jit(solution)/shard_map/pallas_call | solution.py:521

commit v4 on v3

--- a/solution.py
+++ b/solution.py
@@ -11,6 +11,7 @@
 D = 768
 BLOCK = 256
 ROWS = 2048
+LAST = 3
 LOG2E = 1.4426950408889634
 SCALE = 2.0 / math.sqrt(D) * LOG2E
 MESH = pl.DeviceIdType.MESH
@@ -59,15 +60,14 @@
     ("I0",),
     ("B5",),
     ("C0",),
-    ("F3",),
     ("H2",),
     ("B6",),
     ("C1",),
+    ("H3",),
     ("B7",),
     ("C2",),
     ("I1",),
     ("C3",),
-    ("H3",),
     ("I2",),
     ("C4",),
     ("C5",),
@@ -81,7 +81,7 @@
     s_hbm, t_hbm, sp_ref, tp_ref, ids_ref, cnt_ref, gs_out, gt_out,
     s_v, t_v, plan, bias,
     z_part, z_send, z_recv, z2_send, z2_recv, z_out,
-    t_part, c_send, c_recv, x_send, x_recv, y_part, y_send, y_recv, g_out,
+    t_part, c_send, c_recv, x_send, x_recv, y_part, y_send, y_recv, y_all, g_out,
     load_sem, zs, zr, zo, cs, cr, xs, xr, ys, yr, ags, agr, ls, ks, kr,
 ):
     src = lax.axis_index("src")
@@ -294,6 +294,11 @@
                 x_copy(c, p, d).start()
 
     def y_copy(c, p, d):
+        if c == LAST:
+            mine = y_all.at[p, second_of(p)]
+            return remote(
+                mine, mine, ys.at[c, p, d - 1], yr.at[c, p, d - 1], along(1 - p, d)
+            )
         piece = (second_of(p) + d) % 4
         return remote(
             y_send.at[c, p, rows_at(piece * 16, 16)], y_recv.at[c, p, d - 1],
@@ -312,6 +317,9 @@
                 + x_recv[c, p, 1].astype(F32)
                 + x_recv[c, p, 2].astype(F32)
             )
+            if c == LAST:
+                y_all[p, second_of(p)] = total.astype(BF16)
+                continue
             y_part[c, p] = total
             y_send[c, p] = total.astype(BF16)
 
@@ -371,7 +379,16 @@
     def h_wait(c):
         for p in range(2):
             for d in (1, 2, 3):
-                y_gather(c, p, d).wait_recv()
+                (y_copy if c == LAST else y_gather)(c, p, d).wait_recv()
+
+    def h_body(c):
+        if c == LAST:
+            for p in range(2):
+                total = (
+                    y_all[p, 0].astype(F32) + y_all[p, 1].astype(F32)
+                    + y_all[p, 2].astype(F32) + y_all[p, 3].astype(F32)
+                )
+                g_out[c, rows_at(first_of(p) * 64, 64), cols_of(p)] = total.astype(BF16)
 
     def h_start(c):
         for d in (2, 1, 3):
@@ -379,7 +396,7 @@
                 a_copy(c, p, d).start()
         for p in range(2):
             for d in (1, 2, 3):
-                y_gather(c, p, d).wait_send()
+                (y_copy if c == LAST else y_gather)(c, p, d).wait_send()
 
     def i_start(c):
         for p in range(2):
@@ -408,7 +425,7 @@
         "X": (x_wait, x_body, x_start),
         "Y": (y_wait, y_body, y_start),
         "F": (f_wait, f_body, f_start),
-        "H": (h_wait, nothing, h_start),
+        "H": (h_wait, h_body, h_start),
         "I": (nothing, nothing, i_start),
     }
     for copy in loads[:5]:
@@ -487,6 +504,7 @@
             pltpu.VMEM((4, 2, 64, 384), F32),
             pltpu.VMEM((4, 2, 64, 384), BF16),
             pltpu.VMEM((4, 2, 3, 16, 384), BF16),
+            pltpu.VMEM((2, 4, 64, 384), BF16),
             pltpu.VMEM((4, 256, D), BF16),
             dma((6,)),
             dma((8, 4)),

time: 59.4 us -> 58 us (0.976)
  Pallas kernels: 58.4 us -> 57 us
    pallas_call x1, Pallas kernels: 55 us -> 53.6 us  [shards(): pl.pallas_call(kernel, out_shape=(jax.ShapeDtypeStruct((D // 4, ROWS), BF...]
where the time goes in v4:
time: 58 us; the launch traced here: 57.8 us
  Pallas kernels  57 us (98%)
  between operations  0.8 us (1%)
    pallas_call x1, Pallas kernels, shards(): pl.pallas_call(kernel, out_shape=(jax.ShapeDtypeStruct((D // 4, ROWS), BF...  53.6 us
    pallas_call x1, Pallas kernels, shards(): pl.pallas_call(finish, out_shape=(jax.ShapeDtypeStruct((D // 4, ROWS), BF...  3.41 us

profile of v4, /device:TPU:1, one launch (start us, length us, event | category | flops | bytes accessed | tf_op | source)
XLA Modules:
  0.0 57.8 jit_solution(10755193237138647134)
XLA Ops:
  0.6 53.6 %shard_map.77 = (bf16[192,2048]{1,0:T(8,128)(2,1)}, bf16[2048,768]{1,0:T(8,128)(2,1)}) custom-call(bf16[2048,768]{1,0:T(8,128)(2,1)} %s_hbm.1, bf16[2048,768]{1,0:T(8,128)(2,1)} %t_hbm.1, f32[16,128]{1,0:T(8,128)} %bitcast.5, f32[64,128]{1,0:T(8,128)} %bitcast.4, s32[8,24]{1,0:T(8,128)} %ids_ref.1, s32[8]{0:T(128)} %cnt_ref.1), custom_call_target="tpu_custom_call" | custom-call | flops 19327352832 | bytes 12582912 | tf_op jit(solution)/shard_map/pallas_call | solution.py:480
  54.2 3.4 %shard_map.78 = (bf16[192,2048]{1,0:T(8,128)(2,1)}, bf16[2048,768]{1,0:T(8,128)(2,1)}) custom-call(bf16[192,2048]{1,0:T(8,128)(2,1)} %get-tuple-element.6.gs_in, bf16[2048,768]{1,0:T(8,128)(2,1)} %get-tuple-element.7.gt_in), custom_call_target="tpu_custom_call" | custom-call | tf_op jit(solution)/shard_map/pallas_call | solution.py:539
